TPU v7x, 128 devices: a whole 4x4x4 slice. The times are simulated.
128 devices in a mesh: src: 32 (over x, z, core), tgt: 4 (over y).
Axes of the slice: x: 4, y: 4, z: 4, core: 2. Of those that a mesh axis runs over, the one named last changes fastest.
Arguments:
- source_embed: bfloat16 [16384, 768], P('src'), may hold values from -16 to 16
- target_embed: bfloat16 [8192, 768], P(('tgt', 'src')), may hold values from -6 to 6
- source_mass: float32 [16384], P('src'), may hold values from 0.3 to 3
- target_mass: float32 [8192], P('tgt'), may hold values from 0.3 to 3
Outputs:
- readout: float32 [16384, 768], P('src')
- source_potential: float32 [16384], P('src')
- target_potential: float32 [8192], P('tgt')
All inputs are finite; a program needn't handle non-finite values.
Results may differ from a plain program's by a relative error of at most 0.0028.
Values may be sent and summed in bfloat16 or wider, within the bound.
A program may use at most 64 MiB of HBM per device.

v0:
```python
import math
import jax
import jax.numpy as jnp
from jax import lax
from jax.sharding import PartitionSpec as P

D = 768
ITERS = 3


def block_scores(sources, block, scale):
    return (
        lax.dot_general(
            sources, block, (((1,), (1,)), ((), ())), preferred_element_type=jnp.float32
        )
        * scale
    )


def row_pass(sources, tgt_blocks, potential_g, scale):
    rows = sources.shape[0]

    def advance(carry, items):
        block, shift = items
        scores = block_scores(sources, block, scale) + shift[None, :]
        peak = jnp.maximum(carry[0], jnp.max(scores, axis=1))
        total = carry[1] * jnp.exp(carry[0] - peak) + jnp.sum(
            jnp.exp(scores - peak[:, None]), axis=1
        )
        return ((peak, total), None)

    start = (jnp.full((rows,), -1e30, jnp.float32), jnp.zeros((rows,), jnp.float32))
    return lax.scan(advance, start, (tgt_blocks, potential_g))[0]


def column_pass(sources, tgt_blocks, potential_f, scale):

    def single(block):
        scores = block_scores(sources, block, scale) + potential_f[:, None]
        peak = jnp.max(scores, axis=0)
        return (peak, jnp.sum(jnp.exp(scores - peak[None, :]), axis=0))

    return lax.map(single, tgt_blocks)


def shards(source_embed, target_embed, source_mass, target_mass):
    scale = 2.0 / math.sqrt(D)
    gathered = lax.all_gather(target_embed, "src", axis=0, tiled=True)
    total_rows = gathered.shape[0]
    width = 512
    count = total_rows // width
    tgt_blocks = gathered.reshape(count, width, gathered.shape[1])
    log_a = jnp.log(source_mass)
    log_b = jnp.log(target_mass).reshape(count, width)
    potential_g = jnp.zeros((count, width), jnp.float32)
    potential_f = jnp.zeros(log_a.shape, jnp.float32)
    for step in range(ITERS):
        peak, total = row_pass(source_embed, tgt_blocks, potential_g, scale)
        highest = lax.pmax(peak, "tgt")
        total = lax.psum(total * jnp.exp(peak - highest), "tgt")
        peak = highest
        potential_f = log_a - (peak + jnp.log(total))
        column_peak, column_total = column_pass(source_embed, tgt_blocks, potential_f, scale)
        column_high = lax.pmax(column_peak, "src")
        column_total = lax.psum(column_total * jnp.exp(column_peak - column_high), "src")
        column_peak = column_high
        potential_g = log_b - (column_peak + jnp.log(column_total))
    offset = potential_f - log_a

    def gather_step(carry, items):
        block, shift = items
        weights = jnp.exp(
            block_scores(source_embed, block, scale) + shift[None, :] + offset[:, None]
        )
        numer = carry[0] + jnp.dot(
            weights.astype(jnp.bfloat16), block, preferred_element_type=jnp.float32
        )
        return ((numer, carry[1] + jnp.sum(weights, axis=1)), None)

    rows = source_embed.shape[0]
    start = (jnp.zeros((rows, gathered.shape[1]), jnp.float32), jnp.zeros((rows,), jnp.float32))
    numerator, mass = lax.scan(gather_step, start, (tgt_blocks, potential_g))[0]
    numerator, mass = lax.psum((numerator, mass), "tgt")
    readout = numerator / mass[:, None]
    return (readout, potential_f, potential_g.reshape(total_rows))


def solution(mesh):
    placed = (P("src", None), P(("tgt", "src"), None), P("src"), P("tgt"))
    return jax.shard_map(
        shards,
        mesh=mesh,
        in_specs=placed,
        out_specs=(P("src", None), P("src"), P("tgt")),
        check_vma=False,
    )
```

profile of v0, /device:TPU:1, one launch (start us, length us, event | category | flops | bytes accessed | tf_op | source)
XLA Modules:
  0.0 622.1 jit_solution(17024977472537300388)
XLA Ops:
  8.7 50.4 %all-gather.2.cloned.1.call-done = bf16[2048,768]{1,0:T(8,128)(2,1)} async-done(((bf16[64,768]{1,0:T(8,128)(2,1)}), bf16[2048,768]{1,0:T(8,128)(2,1)}) %all-gather.2.cloned.1.call-update) | async-done | bytes 3145744 | tf_op jit(solution)/shard_map/all_gather | solution.py:48
  59.1 9.0 %while.91 = (s32[]{:T(128)}, f32[512]{0:T(512)S(1)}, f32[512]{0:T(512)S(1)}, bf16[4,512,768]{2,1,0:T(8,128)(2,1)}, bf16[512,768]{1,0:T(8,128)(2,1)}, /*index=5*/s32[]{:T(128)}, s32[]{:T(128)}) while((s32[]{:T(128)}, f32[512]{0:T(512)S(1)}, f32[512]{0:T(512)S(1)}, bf16[4,512,768]{2,1,0:T(8,128)(2,1)}, bf16[512,768]{1,0:T(8,128)(2,1)}, ...), condition=%wide.region_3.4_spmd.clone, body=%wide.region_0.3_spmd.clone.sunk | while | flops 403704320 | bytes 3697240 | solution.py:33
  68.1 8.5 %pmax.42 = f32[512]{0:T(512)S(1)} all-reduce(f32[512]{0:T(512)S(1)} %get-tuple-element.234), channel_id=1, replica_groups=mesh['src'=32,'tgt'=4] {'tgt'}, use_global_device_ids=true, to_apply=%region_4.5 | all-reduce | flops 512 | bytes 4096 | tf_op jit(solution)/shard_map/pmax | solution.py:59
  76.5 6.0 psum.56
  82.6 9.2 %while.88 = (s32[]{:T(128)}, f32[4,512]{1,0:T(4,128)S(1)}, f32[4,512]{1,0:T(4,128)S(1)}, bf16[4,512,768]{2,1,0:T(8,128)(2,1)}, bf16[512,768]{1,0:T(8,128)(2,1)}, /*index=5*/f32[512]{0:T(512)S(1)}, s32[]{:T(128)}, s32[]{:T(128)}) while((s32[]{:T(128)}, f32[4,512]{1,0:T(4,128)S(1)}, f32[4,512]{1,0:T(4,128)S(1)}, ...), condition=%wide.region_9.10_spmd, body=%wide.region_6.9_spmd.sunk | while | flops 403962880 | bytes 3687005 | solution.py:43
  91.8 67.0 %pmax.43 = f32[4,512]{1,0:T(4,128)S(1)} all-reduce(f32[4,512]{1,0:T(4,128)S(1)} %get-tuple-element.236), channel_id=1, replica_groups=mesh['src'=32,'tgt'=4] {'src'}, use_global_device_ids=true, to_apply=%region_10.11 | all-reduce | flops 2048 | bytes 16384 | tf_op jit(solution)/shard_map/pmax | solution.py:64
  158.8 63.7 %psum.57 = f32[4,512]{1,0:T(4,128)S(1)} all-reduce(f32[4,512]{1,0:T(4,128)S(1)} %exponential_multiply_fusion.2), channel_id=1, replica_groups=mesh['src'=32,'tgt'=4] {'src'}, use_global_device_ids=true, to_apply=%region_11.12 | all-reduce | flops 2048 | bytes 16384 | tf_op jit(solution)/shard_map/psum | solution.py:65
  222.6 9.0 %while.92 = (s32[]{:T(128)}, f32[512]{0:T(512)S(1)}, f32[512]{0:T(512)S(1)}, bf16[4,512,768]{2,1,0:T(8,128)(2,1)}, bf16[512,768]{1,0:T(8,128)(2,1)}, /*index=5*/f32[4,512]{1,0:T(4,128)S(1)}, s32[]{:T(128)}, s32[]{:T(128)}) while((s32[]{:T(128)}, f32[512]{0:T(512)S(1)}, f32[512]{0:T(512)S(1)}, bf16[4,512,768]{2,1,0:T(8,128)(2,1)}, ...), condition=%wide.region_15.16_spmd.clone, body=%wide.region_12.15_spmd.clone.sunk | while | flops 403966464 | bytes 3703396 | solution.py:33
  231.6 7.7 %pmax.44 = f32[512]{0:T(512)S(1)} all-reduce(f32[512]{0:T(512)S(1)} %get-tuple-element.238), channel_id=1, replica_groups=mesh['src'=32,'tgt'=4] {'tgt'}, use_global_device_ids=true, to_apply=%region_16.17 | all-reduce | flops 512 | bytes 4096 | tf_op jit(solution)/shard_map/pmax | solution.py:59
  239.3 6.0 psum.58
  245.4 9.2 %while.89 = (s32[]{:T(128)}, f32[4,512]{1,0:T(4,128)S(1)}, f32[4,512]{1,0:T(4,128)S(1)}, bf16[4,512,768]{2,1,0:T(8,128)(2,1)}, bf16[512,768]{1,0:T(8,128)(2,1)}, /*index=5*/f32[512]{0:T(512)S(1)}, s32[]{:T(128)}, s32[]{:T(128)}) while((s32[]{:T(128)}, f32[4,512]{1,0:T(4,128)S(1)}, f32[4,512]{1,0:T(4,128)S(1)}, ...), condition=%wide.region_21.22_spmd, body=%wide.region_18.21_spmd.sunk | while | flops 403962880 | bytes 3687005 | solution.py:43
  254.6 67.4 %pmax.45 = f32[4,512]{1,0:T(4,128)S(1)} all-reduce(f32[4,512]{1,0:T(4,128)S(1)} %get-tuple-element.240), channel_id=1, replica_groups=mesh['src'=32,'tgt'=4] {'src'}, use_global_device_ids=true, to_apply=%region_22.23 | all-reduce | flops 2048 | bytes 16384 | tf_op jit(solution)/shard_map/pmax | solution.py:64
  322.1 63.7 %psum.59 = f32[4,512]{1,0:T(4,128)S(1)} all-reduce(f32[4,512]{1,0:T(4,128)S(1)} %exponential_multiply_fusion.1), channel_id=1, replica_groups=mesh['src'=32,'tgt'=4] {'src'}, use_global_device_ids=true, to_apply=%region_23.24 | all-reduce | flops 2048 | bytes 16384 | tf_op jit(solution)/shard_map/psum | solution.py:65
  385.8 9.0 %while.93 = (s32[]{:T(128)}, f32[512]{0:T(512)S(1)}, f32[512]{0:T(512)S(1)}, bf16[4,512,768]{2,1,0:T(8,128)(2,1)}, bf16[512,768]{1,0:T(8,128)(2,1)}, /*index=5*/f32[4,512]{1,0:T(4,128)S(1)}, s32[]{:T(128)}, s32[]{:T(128)}) while((s32[]{:T(128)}, f32[512]{0:T(512)S(1)}, f32[512]{0:T(512)S(1)}, bf16[4,512,768]{2,1,0:T(8,128)(2,1)}, ...), condition=%wide.region_27.28_spmd.clone, body=%wide.region_24.27_spmd.clone.sunk | while | flops 403966464 | bytes 3703396 | solution.py:33
  394.8 7.7 %pmax.46 = f32[512]{0:T(512)S(1)} all-reduce(f32[512]{0:T(512)S(1)} %get-tuple-element.242), channel_id=1, replica_groups=mesh['src'=32,'tgt'=4] {'tgt'}, use_global_device_ids=true, to_apply=%region_28.29 | all-reduce | flops 512 | bytes 4096 | tf_op jit(solution)/shard_map/pmax | solution.py:59
  402.6 6.0 psum.60
  408.6 9.2 %while.90 = (s32[]{:T(128)}, f32[4,512]{1,0:T(4,128)S(1)}, f32[4,512]{1,0:T(4,128)S(1)}, bf16[4,512,768]{2,1,0:T(8,128)(2,1)}, bf16[512,768]{1,0:T(8,128)(2,1)}, /*index=5*/f32[512]{0:T(512)S(1)}, s32[]{:T(128)}, s32[]{:T(128)}) while((s32[]{:T(128)}, f32[4,512]{1,0:T(4,128)S(1)}, f32[4,512]{1,0:T(4,128)S(1)}, ...), condition=%wide.region_33.34_spmd, body=%wide.region_30.33_spmd.sunk | while | flops 403962880 | bytes 3687005 | solution.py:43
  417.9 67.4 %pmax.47 = f32[4,512]{1,0:T(4,128)S(1)} all-reduce(f32[4,512]{1,0:T(4,128)S(1)} %get-tuple-element.244), channel_id=1, replica_groups=mesh['src'=32,'tgt'=4] {'src'}, use_global_device_ids=true, to_apply=%region_34.35 | all-reduce | flops 2048 | bytes 16384 | tf_op jit(solution)/shard_map/pmax | solution.py:64
  485.3 63.7 %psum.61 = f32[4,512]{1,0:T(4,128)S(1)} all-reduce(f32[4,512]{1,0:T(4,128)S(1)} %exponential_multiply_fusion), channel_id=1, replica_groups=mesh['src'=32,'tgt'=4] {'src'}, use_global_device_ids=true, to_apply=%region_35.36 | all-reduce | flops 2048 | bytes 16384 | tf_op jit(solution)/shard_map/psum | solution.py:65
  549.1 16.6 %while.94 = (s32[]{:T(128)}, f32[512,768]{1,0:T(8,128)S(1)}, f32[512]{0:T(512)S(1)}, bf16[4,512,768]{2,1,0:T(8,128)(2,1)}, bf16[512,768]{1,0:T(8,128)(2,1)}, /*i...) while((s32[]{:T(128)}, f32[512,768]{1,0:T(8,128)S(1)}, f32[512]{0:T(512)S(1)}, ...), condition=%wide.region_38.39_spmd.clone, body=%wide.region_36.38_spmd.clone.sunk | while | flops 807404032 | bytes 6571116 | solution.py:82
  553.2 2.1 fusion.88
  567.4 8.6 %psum.63 = f32[512]{0:T(512)S(1)} all-reduce(f32[512]{0:T(512)S(1)} %get-tuple-element.247), channel_id=1, replica_groups=mesh['src'=32,'tgt'=4] {'tgt'}, use_global_device_ids=true, to_apply=%region_40.41 | all-reduce | flops 512 | bytes 4096 | tf_op jit(solution)/shard_map/psum | solution.py:83
  576.0 36.6 %all-reduce.2.cloned.1.call-done = f32[512,768]{1,0:T(8,128)} async-done(((f32[512,768]{1,0:T(8,128)}), f32[512,768]{1,0:T(8,128)}) %all-reduce.2.cloned.1.call-update) | async-done | bytes 1572880 | tf_op jit(solution)/shard_map/psum | solution.py:83
  612.6 2.7 broadcast_divide_fusion
  (170 shorter events, 71.7 us)
Async XLA Ops:
  7.2 51.9 %all-gather.2.cloned.1.call-start = ((), (), s32[]{:S(2)}) async-start(), calls=%async_computation | async-start | bytes 3244032 | tf_op jit(solution)/shard_map/all_gather | solution.py:48
  7.9 604.7 %all-reduce.2.cloned.1.call-start = ((), (), s32[]{:S(2)}) async-start(), calls=%async_computation.1 | async-start | bytes 3145728 | tf_op jit(solution)/shard_map/psum | solution.py:83
  59.1 23.4 %copy-start.1 = (f32[512]{0:T(512)S(1)}, f32[512]{0:T(512)}, u32[]{:S(2)}) copy-start(f32[512]{0:T(512)} %param.20) | copy-start | bytes 6148
  417.9 131.2 %copy-start.2 = (f32[512]{0:T(512)}, f32[512]{0:T(512)S(1)}, u32[]{:S(2)}) copy-start(f32[512]{0:T(512)S(1)} %get-tuple-element.904) | copy-start | bytes 6148
  565.6 1.1 copy-start
Sparse Core Ops, SparseCore 0:
  10.3 48.8 all-gather.1
  566.9 45.5 all-reduce.1
where the time goes:
time: 623 us; the launch traced here: 622 us
  blocking collectives  443 us (71%)
  waiting for transfers between devices  87.7 us (14%)
  matrix products  64.1 us (10%)
  between operations  14.3 us (2%)
  other arithmetic  7.88 us (1%)
    pmax x3, blocking collectives, shards(): column_high = lax.pmax(column_peak, 'src')  202 us
    psum x3, blocking collectives, shards(): lax.psum(column_total * jnp.exp(column_peak - column_high), 'src')  191 us
    dot_general x28, matrix products, block_scores(): lax.dot_general(sources, block, (((1,), (1,)), ((), ())), preferred_eleme...  56.1 us
    all_gather x1, waiting for transfers between devices, shards(): gathered = lax.all_gather(target_embed, 'src', axis=0, tiled=True)  50.4 us
    psum x1, waiting for transfers between devices, shards(): numerator, mass = lax.psum((numerator, mass), 'tgt')  36.6 us
    pmax x3, blocking collectives, shards(): highest = lax.pmax(peak, 'tgt')  23.9 us
    psum x3, blocking collectives, shards(): total = lax.psum(total * jnp.exp(peak - highest), 'tgt')  18 us
  transfers between devices with their start and end apart: 2, of which 2 were waited for; matrix products, arithmetic and copies ran while one was open for 0% of the time, Pallas kernels for 0%

commit v1 on v0

--- a/solution.py
+++ b/solution.py
@@ -62,7 +62,9 @@
         potential_f = log_a - (peak + jnp.log(total))
         column_peak, column_total = column_pass(source_embed, tgt_blocks, potential_f, scale)
         column_high = lax.pmax(column_peak, "src")
-        column_total = lax.psum(column_total * jnp.exp(column_peak - column_high), "src")
+        column_total = jnp.sum(
+            lax.all_gather(column_total * jnp.exp(column_peak - column_high), "src"), axis=0
+        )
         column_peak = column_high
         potential_g = log_b - (column_peak + jnp.log(column_total))
     offset = potential_f - log_a

time: 623 us -> 502 us (0.81)
  blocking collectives: 443 us -> 318 us
    psum x3 -> x0, blocking collectives: 191 us -> none  [shards(): lax.psum(column_total * jnp.exp(column_peak - column_high), 'src')]
    all_gather x0 -> x3, blocking collectives: none -> 67.1 us  [shards(): lax.all_gather(column_total * jnp.exp(column_peak - column_high), 'src')]
where the time goes in v1:
time: 502 us; the launch traced here: 500 us
  blocking collectives  318 us (63%)
  waiting for transfers between devices  91.5 us (18%)
  matrix products  64.1 us (13%)
  between operations  14.3 us (3%)
  other arithmetic  8.07 us (2%)
    pmax x3, blocking collectives, shards(): column_high = lax.pmax(column_peak, 'src')  201 us
    all_gather x3, blocking collectives, shards(): lax.all_gather(column_total * jnp.exp(column_peak - column_high), 'src')  67.1 us
    dot_general x28, matrix products, block_scores(): lax.dot_general(sources, block, (((1,), (1,)), ((), ())), preferred_eleme...  56.1 us
    all_gather x1, waiting for transfers between devices, shards(): gathered = lax.all_gather(target_embed, 'src', axis=0, tiled=True)  50.4 us
    psum x1, waiting for transfers between devices, shards(): numerator, mass = lax.psum((numerator, mass), 'tgt')  40.4 us
    pmax x3, blocking collectives, shards(): highest = lax.pmax(peak, 'tgt')  23.9 us
    psum x3, blocking collectives, shards(): total = lax.psum(total * jnp.exp(peak - highest), 'tgt')  18 us
  transfers between devices with their start and end apart: 2, of which 2 were waited for; matrix products, arithmetic and copies ran while one was open for 0% of the time, Pallas kernels for 0%

profile of v1, /device:TPU:1, one launch (start us, length us, event | category | flops | bytes accessed | tf_op | source)
XLA Modules:
  0.0 500.2 jit_solution(6522222362852981781)
XLA Ops:
  8.7 50.4 %all-gather.8.cloned.1.call-done = bf16[2048,768]{1,0:T(8,128)(2,1)} async-done(((bf16[64,768]{1,0:T(8,128)(2,1)}), bf16[2048,768]{1,0:T(8,128)(2,1)}) %all-gather.8.cloned.1.call-update) | async-done | bytes 3145744 | tf_op jit(solution)/shard_map/all_gather | solution.py:48
  59.1 9.0 %while.91 = (s32[]{:T(128)}, f32[512]{0:T(512)S(1)}, f32[512]{0:T(512)S(1)}, bf16[4,512,768]{2,1,0:T(8,128)(2,1)}, bf16[512,768]{1,0:T(8,128)(2,1)}, /*index=5*/s32[]{:T(128)}, s32[]{:T(128)}) while((s32[]{:T(128)}, f32[512]{0:T(512)S(1)}, f32[512]{0:T(512)S(1)}, bf16[4,512,768]{2,1,0:T(8,128)(2,1)}, bf16[512,768]{1,0:T(8,128)(2,1)}, ...), condition=%wide.region_3.4_spmd.clone, body=%wide.region_0.3_spmd.clone.sunk | while | flops 403704320 | bytes 3697240 | solution.py:33
  68.1 8.5 %pmax.42 = f32[512]{0:T(512)S(1)} all-reduce(f32[512]{0:T(512)S(1)} %get-tuple-element.234), channel_id=1, replica_groups=mesh['src'=32,'tgt'=4] {'tgt'}, use_global_device_ids=true, to_apply=%region_4.5 | all-reduce | flops 512 | bytes 4096 | tf_op jit(solution)/shard_map/pmax | solution.py:59
  76.5 6.0 %psum.35 = f32[512]{0:T(512)S(1)} all-reduce(f32[512]{0:T(512)S(1)} %exponential_multiply_fusion.2), channel_id=1, replica_groups=mesh['src'=32,'tgt'=4] {'tgt'}, use_global_device_ids=true, to_apply=%region_5.6 | all-reduce | flops 512 | bytes 4096 | tf_op jit(solution)/shard_map/psum | solution.py:60
  82.6 9.2 %while.88 = (s32[]{:T(128)}, f32[4,512]{1,0:T(4,128)S(1)}, f32[4,512]{1,0:T(4,128)S(1)}, bf16[4,512,768]{2,1,0:T(8,128)(2,1)}, bf16[512,768]{1,0:T(8,128)(2,1)}, /*index=5*/f32[512]{0:T(512)S(1)}, s32[]{:T(128)}, s32[]{:T(128)}) while((s32[]{:T(128)}, f32[4,512]{1,0:T(4,128)S(1)}, f32[4,512]{1,0:T(4,128)S(1)}, ...), condition=%wide.region_9.10_spmd, body=%wide.region_6.9_spmd.sunk | while | flops 403962880 | bytes 3687005 | solution.py:43
  91.8 67.0 %pmax.43 = f32[4,512]{1,0:T(4,128)S(1)} all-reduce(f32[4,512]{1,0:T(4,128)S(1)} %get-tuple-element.236), channel_id=1, replica_groups=mesh['src'=32,'tgt'=4] {'src'}, use_global_device_ids=true, to_apply=%region_10.11 | all-reduce | flops 2048 | bytes 16384 | tf_op jit(solution)/shard_map/pmax | solution.py:64
  158.8 22.4 %all-gather.3 = f32[32,4,512]{2,1,0:T(4,128)S(1)} all-gather(f32[1,4,512]{2,1,0:T(4,128)S(1)} %multiply_bitcast_fusion.2), channel_id=2, replica_groups=mesh['src'=32,'tgt'=4] {'src'}, dimensions={0}, use_global_device_ids=true | all-gather | bytes 270336 | tf_op jit(solution)/shard_map/all_gather | solution.py:66
  181.3 9.0 %while.92 = (s32[]{:T(128)}, f32[512]{0:T(512)S(1)}, f32[512]{0:T(512)S(1)}, bf16[4,512,768]{2,1,0:T(8,128)(2,1)}, bf16[512,768]{1,0:T(8,128)(2,1)}, /*index=5*/f32[4,512]{1,0:T(4,128)S(1)}, s32[]{:T(128)}, s32[]{:T(128)}) while((s32[]{:T(128)}, f32[512]{0:T(512)S(1)}, f32[512]{0:T(512)S(1)}, bf16[4,512,768]{2,1,0:T(8,128)(2,1)}, ...), condition=%wide.region_15.16_spmd.clone, body=%wide.region_12.15_spmd.clone.sunk | while | flops 403966464 | bytes 3703396 | solution.py:33
  190.3 7.7 %pmax.44 = f32[512]{0:T(512)S(1)} all-reduce(f32[512]{0:T(512)S(1)} %get-tuple-element.238), channel_id=1, replica_groups=mesh['src'=32,'tgt'=4] {'tgt'}, use_global_device_ids=true, to_apply=%region_16.17 | all-reduce | flops 512 | bytes 4096 | tf_op jit(solution)/shard_map/pmax | solution.py:59
  198.1 6.0 %psum.36 = f32[512]{0:T(512)S(1)} all-reduce(f32[512]{0:T(512)S(1)} %exponential_multiply_fusion.1), channel_id=1, replica_groups=mesh['src'=32,'tgt'=4] {'tgt'}, use_global_device_ids=true, to_apply=%region_17.18 | all-reduce | flops 512 | bytes 4096 | tf_op jit(solution)/shard_map/psum | solution.py:60
  204.1 9.2 %while.89 = (s32[]{:T(128)}, f32[4,512]{1,0:T(4,128)S(1)}, f32[4,512]{1,0:T(4,128)S(1)}, bf16[4,512,768]{2,1,0:T(8,128)(2,1)}, bf16[512,768]{1,0:T(8,128)(2,1)}, /*index=5*/f32[512]{0:T(512)S(1)}, s32[]{:T(128)}, s32[]{:T(128)}) while((s32[]{:T(128)}, f32[4,512]{1,0:T(4,128)S(1)}, f32[4,512]{1,0:T(4,128)S(1)}, ...), condition=%wide.region_21.22_spmd, body=%wide.region_18.21_spmd.sunk | while | flops 403962880 | bytes 3687005 | solution.py:43
  213.3 66.9 %pmax.45 = f32[4,512]{1,0:T(4,128)S(1)} all-reduce(f32[4,512]{1,0:T(4,128)S(1)} %get-tuple-element.240), channel_id=1, replica_groups=mesh['src'=32,'tgt'=4] {'src'}, use_global_device_ids=true, to_apply=%region_22.23 | all-reduce | flops 2048 | bytes 16384 | tf_op jit(solution)/shard_map/pmax | solution.py:64
  280.3 22.4 %all-gather.4 = f32[32,4,512]{2,1,0:T(4,128)S(1)} all-gather(f32[1,4,512]{2,1,0:T(4,128)S(1)} %multiply_bitcast_fusion.1), channel_id=3, replica_groups=mesh['src'=32,'tgt'=4] {'src'}, dimensions={0}, use_global_device_ids=true | all-gather | bytes 270336 | tf_op jit(solution)/shard_map/all_gather | solution.py:66
  302.7 9.0 %while.93 = (s32[]{:T(128)}, f32[512]{0:T(512)S(1)}, f32[512]{0:T(512)S(1)}, bf16[4,512,768]{2,1,0:T(8,128)(2,1)}, bf16[512,768]{1,0:T(8,128)(2,1)}, /*index=5*/f32[4,512]{1,0:T(4,128)S(1)}, s32[]{:T(128)}, s32[]{:T(128)}) while((s32[]{:T(128)}, f32[512]{0:T(512)S(1)}, f32[512]{0:T(512)S(1)}, bf16[4,512,768]{2,1,0:T(8,128)(2,1)}, ...), condition=%wide.region_27.28_spmd.clone, body=%wide.region_24.27_spmd.clone.sunk | while | flops 403966464 | bytes 3703396 | solution.py:33
  311.8 7.7 %pmax.46 = f32[512]{0:T(512)S(1)} all-reduce(f32[512]{0:T(512)S(1)} %get-tuple-element.242), channel_id=1, replica_groups=mesh['src'=32,'tgt'=4] {'tgt'}, use_global_device_ids=true, to_apply=%region_28.29 | all-reduce | flops 512 | bytes 4096 | tf_op jit(solution)/shard_map/pmax | solution.py:59
  319.5 6.0 %psum.37 = f32[512]{0:T(512)S(1)} all-reduce(f32[512]{0:T(512)S(1)} %exponential_multiply_fusion), channel_id=1, replica_groups=mesh['src'=32,'tgt'=4] {'tgt'}, use_global_device_ids=true, to_apply=%region_29.30 | all-reduce | flops 512 | bytes 4096 | tf_op jit(solution)/shard_map/psum | solution.py:60
  325.5 9.2 %while.90 = (s32[]{:T(128)}, f32[4,512]{1,0:T(4,128)S(1)}, f32[4,512]{1,0:T(4,128)S(1)}, bf16[4,512,768]{2,1,0:T(8,128)(2,1)}, bf16[512,768]{1,0:T(8,128)(2,1)}, /*index=5*/f32[512]{0:T(512)S(1)}, s32[]{:T(128)}, s32[]{:T(128)}) while((s32[]{:T(128)}, f32[4,512]{1,0:T(4,128)S(1)}, f32[4,512]{1,0:T(4,128)S(1)}, ...), condition=%wide.region_33.34_spmd, body=%wide.region_30.33_spmd.sunk | while | flops 403962880 | bytes 3687005 | solution.py:43
  334.8 66.9 %pmax.47 = f32[4,512]{1,0:T(4,128)S(1)} all-reduce(f32[4,512]{1,0:T(4,128)S(1)} %get-tuple-element.244), channel_id=1, replica_groups=mesh['src'=32,'tgt'=4] {'src'}, use_global_device_ids=true, to_apply=%region_34.35 | all-reduce | flops 2048 | bytes 16384 | tf_op jit(solution)/shard_map/pmax | solution.py:64
  401.7 22.4 %all-gather.5 = f32[32,4,512]{2,1,0:T(4,128)S(1)} all-gather(f32[1,4,512]{2,1,0:T(4,128)S(1)} %multiply_bitcast_fusion), channel_id=4, replica_groups=mesh['src'=32,'tgt'=4] {'src'}, dimensions={0}, use_global_device_ids=true | all-gather | bytes 270336 | tf_op jit(solution)/shard_map/all_gather | solution.py:66
  424.2 16.6 %while.94 = (s32[]{:T(128)}, f32[512,768]{1,0:T(8,128)S(1)}, f32[512]{0:T(512)S(1)}, bf16[4,512,768]{2,1,0:T(8,128)(2,1)}, bf16[512,768]{1,0:T(8,128)(2,1)}, /*i...) while((s32[]{:T(128)}, f32[512,768]{1,0:T(8,128)S(1)}, f32[512]{0:T(512)S(1)}, ...), condition=%wide.region_38.39_spmd.clone, body=%wide.region_36.38_spmd.clone.sunk | while | flops 807404032 | bytes 6571116 | solution.py:84
  428.4 2.1 fusion.88
  442.5 7.7 %psum.39 = f32[512]{0:T(512)S(1)} all-reduce(f32[512]{0:T(512)S(1)} %get-tuple-element.247), channel_id=1, replica_groups=mesh['src'=32,'tgt'=4] {'tgt'}, use_global_device_ids=true, to_apply=%region_40.41 | all-reduce | flops 512 | bytes 4096 | tf_op jit(solution)/shard_map/psum | solution.py:85
  450.2 40.4 %all-reduce.2.cloned.1.call-done = f32[512,768]{1,0:T(8,128)} async-done(((f32[512,768]{1,0:T(8,128)}), f32[512,768]{1,0:T(8,128)}) %all-reduce.2.cloned.1.call-update) | async-done | bytes 1572880 | tf_op jit(solution)/shard_map/psum | solution.py:85
  490.7 2.7 broadcast_divide_fusion
  (173 shorter events, 71.9 us)
Async XLA Ops:
  7.2 51.9 %all-gather.8.cloned.1.call-start = ((), (), s32[]{:S(2)}) async-start(), calls=%async_computation | async-start | bytes 3244032 | tf_op jit(solution)/shard_map/all_gather | solution.py:48
  7.9 482.8 %all-reduce.2.cloned.1.call-start = ((), (), s32[]{:S(2)}) async-start(), calls=%async_computation.1 | async-start | bytes 3145728 | tf_op jit(solution)/shard_map/psum | solution.py:85
  59.1 23.4 %copy-start.1 = (f32[512]{0:T(512)S(1)}, f32[512]{0:T(512)}, u32[]{:S(2)}) copy-start(f32[512]{0:T(512)} %param.20) | copy-start | bytes 6148
  334.8 89.4 %copy-start.2 = (f32[512]{0:T(512)}, f32[512]{0:T(512)S(1)}, u32[]{:S(2)}) copy-start(f32[512]{0:T(512)S(1)} %get-tuple-element.904) | copy-start | bytes 6148
  440.8 1.1 copy-start
Sparse Core Ops, SparseCore 0:
  10.3 48.8 all-gather.7
  442.1 48.5 all-reduce.1
